TPU v7x, 32 devices: a whole 2x2x4 slice. The times are simulated.
32 devices in a mesh: group: 2 (over y), cell: 8 (over z, x), head: 2 (over core).
Axes of the slice: x: 2, y: 2, z: 4, core: 2. Of those that a mesh axis runs over, the one named last changes fastest.
Arguments:
- latents: bfloat16 [4096, 1024], P(('group', 'cell')), parts along dimension 0, may hold values from -6.2 to 6.2
- cells: bfloat16 [16384, 1024], P(('group', 'cell')), parts along dimension 0, may hold values from -6 to 6
- w_query: bfloat16 [1024, 1024], P(None, 'head'), may hold values from -1.53125 to 1.53125
- w_key: bfloat16 [1024, 1024], P(None, 'head'), may hold values from -0.134375 to 0.134375
- w_value: bfloat16 [1024, 1024], P(None, 'head'), may hold values from -0.1875 to 0.1875
- w_out: bfloat16 [1024, 1024], replicated, may hold values from -0.1875 to 0.1875
- w_up: bfloat16 [1024, 4096], P(None, ('cell', 'head')), may hold values from -0.1875 to 0.1875
- w_down: bfloat16 [4096, 1024], P(('cell', 'head')), may hold values from -0.09375 to 0.09375
Outputs:
- prototypes: bfloat16 [4096, 1024], P(('group', 'cell', 'head')), parts along dimension 0
There are 2 independent parts, one for each index of `group`. A program takes and returns all parts, laid end to end along the dimension named above; an argument that names none is the same for every part. Nothing has to cross between parts.
All inputs are finite; a program needn't handle non-finite values.
Results may differ from a plain program's by a relative error of at most 0.015.
Values may be sent and summed in bfloat16 or wider, within the bound.
A program may use at most 128 MiB of HBM per device.

v0:
```python
import jax
import jax.numpy as jnp
from jax import lax
from jax.sharding import PartitionSpec as P

HEAD_DIM = 64


def pair_slice(matrix, pair_index, pair_width):
    return lax.dynamic_slice_in_dim(matrix, pair_index * pair_width, pair_width, 1)


def body(latents, cells, w_query, w_key, w_value, w_out, w_up, w_down):
    factor = HEAD_DIM ** (-0.5)
    pair_width = 2 * HEAD_DIM
    key_rows = jnp.dot(cells, w_key, preferred_element_type=jnp.float32).astype(jnp.bfloat16)
    value_rows = jnp.dot(cells, w_value, preferred_element_type=jnp.float32).astype(jnp.bfloat16)
    local_queries = jnp.dot(latents, w_query, preferred_element_type=jnp.float32).astype(
        jnp.bfloat16
    )
    queries = lax.all_gather(local_queries, "cell", axis=0, tiled=True)
    latent_count = queries.shape[0]
    cell_count = cells.shape[0]
    pair_count = w_query.shape[1] // pair_width
    pair_ids = jnp.arange(pair_count, dtype=jnp.int32)

    def pair_partial(pair_index):
        query_pair = pair_slice(queries, pair_index, pair_width).reshape(latent_count, 2, HEAD_DIM)
        key_pair = pair_slice(key_rows, pair_index, pair_width).reshape(cell_count, 2, HEAD_DIM)
        scores = (
            jnp.einsum("lhd,chd->hlc", query_pair, key_pair, preferred_element_type=jnp.float32)
            * factor
        )
        block_max = jnp.max(scores, axis=2)
        weights = jnp.exp(scores - block_max[:, :, None])
        totals = jnp.sum(weights, axis=2)
        value_pair = pair_slice(value_rows, pair_index, pair_width).reshape(cell_count, 2, HEAD_DIM)
        summed = jnp.einsum(
            "hlc,chd->lhd",
            weights.astype(jnp.bfloat16),
            value_pair,
            preferred_element_type=jnp.float32,
        )
        return (summed.reshape(latent_count, pair_width), totals, block_max)

    partial_out, partial_tot, block_max = lax.map(pair_partial, pair_ids)
    maxima = lax.pmax(block_max.astype(jnp.bfloat16), "cell").astype(block_max.dtype)
    shrink = jnp.exp(block_max - maxima)
    scaled_out = (
        partial_out.reshape(pair_count, latent_count, 2, HEAD_DIM)
        * jnp.transpose(shrink, (0, 2, 1))[:, :, :, None]
    )
    scaled_out = scaled_out.reshape(pair_count, latent_count, pair_width)
    scaled_tot = partial_tot * shrink
    rows_cell = latent_count // lax.axis_size("cell")
    summed_out, summed_tot = lax.psum((scaled_out, scaled_tot), "cell")
    first_row = lax.axis_index("cell") * rows_cell
    summed_out = lax.dynamic_slice_in_dim(summed_out, first_row, rows_cell, 1)
    summed_tot = lax.dynamic_slice_in_dim(summed_tot, first_row, rows_cell, 2)
    ratios = (
        summed_out.reshape(pair_count, rows_cell, 2, HEAD_DIM)
        / jnp.transpose(summed_tot, (0, 2, 1))[:, :, :, None]
    )
    attended = (
        jnp.transpose(ratios, (1, 0, 2, 3))
        .reshape(rows_cell, pair_count * pair_width)
        .astype(jnp.bfloat16)
    )
    half_rows = rows_cell // lax.axis_size("head")
    own_latents = lax.dynamic_slice_in_dim(
        latents, lax.axis_index("head") * half_rows, half_rows, 0
    )
    all_heads = lax.all_to_all(attended, "head", split_axis=0, concat_axis=1, tiled=True)
    projected = jnp.dot(all_heads, w_out, preferred_element_type=jnp.float32)
    updated = (own_latents.astype(jnp.float32) + projected).astype(jnp.bfloat16)
    widened = updated.astype(jnp.float32)
    normed = (
        widened * lax.rsqrt(jnp.mean(widened * widened, axis=1, keepdims=True) + 1e-05)
    ).astype(jnp.bfloat16)
    hidden = jax.nn.gelu(
        jnp.dot(
            normed,
            lax.all_gather(w_up, ("cell", "head"), axis=1, tiled=True),
            preferred_element_type=jnp.float32,
        ),
        approximate=True,
    ).astype(jnp.bfloat16)
    mlp_out = jnp.dot(
        hidden,
        lax.all_gather(w_down, ("cell", "head"), axis=0, tiled=True),
        preferred_element_type=jnp.float32,
    )
    return (widened + mlp_out).astype(jnp.bfloat16)


def solution(mesh):
    return jax.shard_map(
        body,
        mesh=mesh,
        in_specs=(
            P(("group", "cell"), None),
            P(("group", "cell"), None),
            P(None, "head"),
            P(None, "head"),
            P(None, "head"),
            P(),
            P(None, ("cell", "head")),
            P(("cell", "head"), None),
        ),
        out_specs=P(("group", "cell", "head"), None),
        check_vma=False,
    )
```

profile of v0, /device:TPU:0, one launch (start us, length us, event | category | flops | bytes accessed | tf_op | source)
XLA Modules:
  0.0 472.8 jit_solution(204552376012297400)
XLA Ops:
  7.4 2.7 convolution_convert_fusion.2
  10.2 3.6 convolution_convert_fusion
  13.7 2.2 convolution_convert_fusion.1
  16.0 46.4 %all-gather.4.cloned.1.call-done = bf16[2048,512]{1,0:T(8,128)(2,1)} async-done(((bf16[256,512]{1,0:T(8,128)(2,1)}), bf16[2048,512]{1,0:T(8,128)(2,1)}) %all-gather.4.cloned.1.call-update) | async-done | bytes 2097168 | tf_op jit(solution)/shard_map/all_gather | solution.py:21
  62.3 119.4 %while.14 = (s32[]{:T(128)}, f32[4,2048,128]{1,2,0:T(8,128)}, f32[4,2,2048]{2,1,0:T(2,128)S(1)}, f32[4,2,2048]{2,1,0:T(2,128)S(1)}, s32[4]{0:T(128)S(1)}, /*inde...) while((s32[]{:T(128)}, f32[4,2048,128]{1,2,0:T(8,128)}, ...), condition=%wide.region_3.4_spmd, body=%wide.region_0.3_spmd.sunk | while | flops 1107288064 | bytes 58852028 | solution.py:46
  62.3 0.6 dynamic_slice.38
  63.6 1.1 constant_dynamic-slice_fusion.8
  64.9 1.0 constant_dynamic-slice_fusion.9
  66.0 8.1 %multiply_reduce_fusion.3 = (f32[2,2048]{1,0:T(2,128)S(1)}, f32[2,2048,1024]{1,2,0:T(8,128)}) fusion(bf16[2048,2,64]{0,2,1:T(8,128)(2,1)S(1)} %bitcast.59, bf16[1024,2,64]{0,2,1:T(8,128)(2,1)S(1)} %bitcast.60), kind=kOutput, calls=%fused_computation.1.clone.1 | convolution fusion | flops 545255424 | bytes 17580032 | tf_op jit(solution)/shard_map/while/body/eval_jaxpr/lhd,chd->hlc/dot_general | solution.py:31
  74.1 8.5 %fusion.55 = f32[2,2048]{1,0:T(2,128)S(1)} fusion(f32[2,2048,1024]{1,2,0:T(8,128)} %get-tuple-element.163, f32[2,2048]{1,0:T(2,128)S(1)} %get-tuple-element.164), kind=kLoop, calls=%fused_computation.2.clone.1 | loop fusion | flops 12578816 | bytes 16809984 | tf_op jit(solution)/shard_map/while/body/eval_jaxpr/reduce_sum | solution.py:36
  82.7 1.0 constant_dynamic-slice_fusion.7
  83.8 7.3 %fusion.54 = f32[2,64,2048]{2,1,0:T(8,128)S(1)} fusion(bf16[1024,2,64]{0,2,1:T(8,128)(2,1)S(1)} %bitcast.61, f32[2,2048,1024]{1,2,0:T(8,128)} %get-tuple-element.163, f32[2,2048]{1,0:T(2,128)S(1)} %get-tuple-element.164), kind=kOutput, calls=%fused_computation.4.clone.1 | convolution fusion | flops 549453824 | bytes 18104320 | tf_op jit(solution)/shard_map/while/body/eval_jaxpr/hlc,chd->lhd/dot_general | solution.py:38
  91.1 1.1 constant_dynamic-update-slice_fusion.2
  92.2 0.6 dynamic_slice.38
  93.4 1.1 constant_dynamic-slice_fusion.8
  94.7 1.0 constant_dynamic-slice_fusion.9
  95.8 8.1 %multiply_reduce_fusion.3 = (f32[2,2048]{1,0:T(2,128)S(1)}, f32[2,2048,1024]{1,2,0:T(8,128)}) fusion(bf16[2048,2,64]{0,2,1:T(8,128)(2,1)S(1)} %bitcast.59, bf16[1024,2,64]{0,2,1:T(8,128)(2,1)S(1)} %bitcast.60), kind=kOutput, calls=%fused_computation.1.clone.1 | convolution fusion | flops 545255424 | bytes 17580032 | tf_op jit(solution)/shard_map/while/body/eval_jaxpr/lhd,chd->hlc/dot_general | solution.py:31
  104.0 8.5 %fusion.55 = f32[2,2048]{1,0:T(2,128)S(1)} fusion(f32[2,2048,1024]{1,2,0:T(8,128)} %get-tuple-element.163, f32[2,2048]{1,0:T(2,128)S(1)} %get-tuple-element.164), kind=kLoop, calls=%fused_computation.2.clone.1 | loop fusion | flops 12578816 | bytes 16809984 | tf_op jit(solution)/shard_map/while/body/eval_jaxpr/reduce_sum | solution.py:36
  112.5 1.0 constant_dynamic-slice_fusion.7
  113.6 7.3 %fusion.54 = f32[2,64,2048]{2,1,0:T(8,128)S(1)} fusion(bf16[1024,2,64]{0,2,1:T(8,128)(2,1)S(1)} %bitcast.61, f32[2,2048,1024]{1,2,0:T(8,128)} %get-tuple-element.163, f32[2,2048]{1,0:T(2,128)S(1)} %get-tuple-element.164), kind=kOutput, calls=%fused_computation.4.clone.1 | convolution fusion | flops 549453824 | bytes 18104320 | tf_op jit(solution)/shard_map/while/body/eval_jaxpr/hlc,chd->lhd/dot_general | solution.py:38
  120.9 1.1 constant_dynamic-update-slice_fusion.2
  122.1 0.6 dynamic_slice.38
  123.3 1.1 constant_dynamic-slice_fusion.8
  124.6 1.0 constant_dynamic-slice_fusion.9
  125.7 8.1 %multiply_reduce_fusion.3 = (f32[2,2048]{1,0:T(2,128)S(1)}, f32[2,2048,1024]{1,2,0:T(8,128)}) fusion(bf16[2048,2,64]{0,2,1:T(8,128)(2,1)S(1)} %bitcast.59, bf16[1024,2,64]{0,2,1:T(8,128)(2,1)S(1)} %bitcast.60), kind=kOutput, calls=%fused_computation.1.clone.1 | convolution fusion | flops 545255424 | bytes 17580032 | tf_op jit(solution)/shard_map/while/body/eval_jaxpr/lhd,chd->hlc/dot_general | solution.py:31
  133.8 8.5 %fusion.55 = f32[2,2048]{1,0:T(2,128)S(1)} fusion(f32[2,2048,1024]{1,2,0:T(8,128)} %get-tuple-element.163, f32[2,2048]{1,0:T(2,128)S(1)} %get-tuple-element.164), kind=kLoop, calls=%fused_computation.2.clone.1 | loop fusion | flops 12578816 | bytes 16809984 | tf_op jit(solution)/shard_map/while/body/eval_jaxpr/reduce_sum | solution.py:36
  142.4 1.0 constant_dynamic-slice_fusion.7
  143.5 7.3 %fusion.54 = f32[2,64,2048]{2,1,0:T(8,128)S(1)} fusion(bf16[1024,2,64]{0,2,1:T(8,128)(2,1)S(1)} %bitcast.61, f32[2,2048,1024]{1,2,0:T(8,128)} %get-tuple-element.163, f32[2,2048]{1,0:T(2,128)S(1)} %get-tuple-element.164), kind=kOutput, calls=%fused_computation.4.clone.1 | convolution fusion | flops 549453824 | bytes 18104320 | tf_op jit(solution)/shard_map/while/body/eval_jaxpr/hlc,chd->lhd/dot_general | solution.py:38
  150.8 1.1 constant_dynamic-update-slice_fusion.2
  151.9 0.6 dynamic_slice.38
  153.1 1.1 constant_dynamic-slice_fusion.8
  154.4 1.0 constant_dynamic-slice_fusion.9
  155.6 8.1 %multiply_reduce_fusion.3 = (f32[2,2048]{1,0:T(2,128)S(1)}, f32[2,2048,1024]{1,2,0:T(8,128)}) fusion(bf16[2048,2,64]{0,2,1:T(8,128)(2,1)S(1)} %bitcast.59, bf16[1024,2,64]{0,2,1:T(8,128)(2,1)S(1)} %bitcast.60), kind=kOutput, calls=%fused_computation.1.clone.1 | convolution fusion | flops 545255424 | bytes 17580032 | tf_op jit(solution)/shard_map/while/body/eval_jaxpr/lhd,chd->hlc/dot_general | solution.py:31
  163.7 8.5 %fusion.55 = f32[2,2048]{1,0:T(2,128)S(1)} fusion(f32[2,2048,1024]{1,2,0:T(8,128)} %get-tuple-element.163, f32[2,2048]{1,0:T(2,128)S(1)} %get-tuple-element.164), kind=kLoop, calls=%fused_computation.2.clone.1 | loop fusion | flops 12578816 | bytes 16809984 | tf_op jit(solution)/shard_map/while/body/eval_jaxpr/reduce_sum | solution.py:36
  172.2 1.0 constant_dynamic-slice_fusion.7
  173.4 7.3 %fusion.54 = f32[2,64,2048]{2,1,0:T(8,128)S(1)} fusion(bf16[1024,2,64]{0,2,1:T(8,128)(2,1)S(1)} %bitcast.61, f32[2,2048,1024]{1,2,0:T(8,128)} %get-tuple-element.163, f32[2,2048]{1,0:T(2,128)S(1)} %get-tuple-element.164), kind=kOutput, calls=%fused_computation.4.clone.1 | convolution fusion | flops 549453824 | bytes 18104320 | tf_op jit(solution)/shard_map/while/body/eval_jaxpr/hlc,chd->lhd/dot_general | solution.py:38
  180.7 1.1 constant_dynamic-update-slice_fusion.2
  181.8 34.7 %pmax.7 = bf16[4,2,2048]{2,1,0:T(2,128)(2,1)S(1)} all-reduce(bf16[4,2,2048]{2,1,0:T(2,128)(2,1)S(1)} %convert_element_type.50), channel_id=1, replica_groups=mesh['group'=2,'cell'=8,'head'=2] {'cell'}, use_global_device_ids=true, to_apply=%region_4.5 | all-reduce | flops 16384 | bytes 65536 | tf_op jit(solution)/shard_map/pmax | solution.py:47
  216.5 0.7 fusion.25
  217.2 4.8 %bitcast_multiply_fusion = f32[4,2048,128]{1,2,0:T(8,128)} fusion(f32[4,2048,128]{1,2,0:T(8,128)} %get-tuple-element.49, f32[4,2048,2]{1,2,0:T(2,128)S(1)} %get-tuple-element.107), kind=kLoop, calls=%fused_computation.12 | loop fusion | flops 1048576 | bytes 8454144 | tf_op jit(solution)/shard_map/mul | solution.py:50
  222.7 0.5 all-gather.8.cloned.1.call-update
  223.2 220.9 %all-reduce.3.cloned.1.call-done = (f32[4,2048,128]{1,2,0:T(8,128)}, f32[4,2,2048]{2,1,0:T(2,128)}) async-done(((f32[4,2048,128]{1,2,0:T(8,128)}, f32[4,2,2048]{2,1,0:T(2,128)}), (f32[4,2048,128]{1,2,0:T(8,128)}, f32[4,2,2048]{2,1,0:T(2,128)})) %all-reduce.3.cloned.1.call-update) | async-done | bytes 4259856 | tf_op jit(solution)/shard_map/psum | solution.py:56
  444.1 0.7 dynamic-slice_bitcast_fusion
  444.8 1.1 constant_dynamic-slice_fusion.3
  446.1 4.0 all_to_all.16
  450.1 2.1 multiply_reduce_fusion.1
  452.3 3.8 all-gather.8.cloned.1.call-done
  456.2 9.2 %fusion.13 = bf16[128,1024]{1,0:T(8,128)(2,1)} fusion(f32[128,1024]{1,0:T(8,128)S(1)} %get-tuple-element.109, bf16[4096,1024]{1,0:T(8,128)(2,1)} %all-gather.8.cloned.1.call-done, bf16[1024,4096]{1,0:T(8,128)(2,1)} %all-gather.6.cloned.1.call-done, f32[128]{0:T(128)S(1)} %add_rsqrt_fusion), kind=kOutput, calls=%fused_computation.26 | convolution fusion | flops 2152726528 | bytes 17564160 | tf_op jit(solution)/shard_map/dot_general | solution.py:88
  (39 shorter events, 3.0 us)
Async XLA Ops:
  7.4 2.8 copy-start
  7.4 55.0 %all-gather.4.cloned.1.call-start = ((), (), s32[]{:S(2)}) async-start(), calls=%async_computation.1 | async-start | bytes 2359296 | tf_op jit(solution)/shard_map/all_gather | solution.py:21
  10.1 434.1 %all-reduce.3.cloned.1.call-start = ((), (), s32[]{:S(2)}) async-start(), calls=%async_computation.4 | async-start | bytes 8519680 | tf_op jit(solution)/shard_map/psum | solution.py:56
  10.2 3.6 copy-start.2
  222.0 228.1 %copy-start.1 = (bf16[256,1024]{1,0:T(8,128)(2,1)S(1)}, bf16[256,1024]{1,0:T(8,128)(2,1)}, u32[]{:S(2)}) copy-start(bf16[256,1024]{1,0:T(8,128)(2,1)} %param.10) | copy-start | bytes 1572868
  222.0 230.3 %all-gather.6.cloned.1.call-start = ((), (), s32[]{:S(2)}) async-start(), calls=%async_computation.2 | async-start | bytes 8912896 | tf_op jit(solution)/shard_map/all_gather | solution.py:83
  222.6 233.6 %all-gather.8.cloned.1.call-start = ((), (), s32[]{:S(2)}) async-start(), calls=%async_computation.3 | async-start | bytes 8912896 | tf_op jit(solution)/shard_map/all_gather | solution.py:90
Sparse Core Ops, SparseCore 0:
  10.3 51.9 all-gather.3
  222.1 221.9 all-reduce.2
Sparse Core Ops, SparseCore 1:
  224.7 118.9 all-gather.5
  345.7 110.4 all-gather.7
where the time goes:
time: 474 us; the launch traced here: 473 us
  waiting for transfers between devices  272 us (57%)
  matrix products  81.5 us (17%)
  other arithmetic  39.7 us (8%)
  blocking collectives  38.7 us (8%)
  local copies, waits for them, and re-layouts  22.8 us (5%)
  between operations  14.9 us (3%)
    psum x1, waiting for transfers between devices, body(): summed_out, summed_tot = lax.psum((scaled_out, scaled_tot), 'cell')  221 us
    all_gather x1, waiting for transfers between devices, body(): queries = lax.all_gather(local_queries, 'cell', axis=0, tiled=True)  46.4 us
    pmax x1, blocking collectives, body(): lax.pmax(block_max.astype(jnp.bfloat16), 'cell').astype(block_max.dtype)  34.7 us
    reduce_sum x4, other arithmetic, pair_partial(): totals = jnp.sum(weights, axis=2)  34 us
    dot_general x4, matrix products, pair_partial(): jnp.einsum('lhd,chd->hlc', query_pair, key_pair, preferred_element_type=j...  32.5 us
    dot_general x4, matrix products, pair_partial(): jnp.einsum('hlc,chd->lhd', weights.astype(jnp.bfloat16), value_pair, pref...  29.2 us
    dynamic_slice x24, local copies, waits for them, and re-layouts, pair_slice(): lax.dynamic_slice_in_dim(matrix, pair_index * pair_width, pair_width, 1)  14.1 us
  transfers between devices with their start and end apart: 4, of which 3 were waited for; matrix products, arithmetic and copies ran while one was open for 2% of the time, Pallas kernels for 0%

commit v1 on v0

v1 whole, which is shorter than its diff:
```python
import functools
import math

import jax
import jax.numpy as jnp
from jax import lax
from jax.experimental import pallas as pl
from jax.experimental.pallas import tpu as pltpu
from jax.sharding import PartitionSpec as P

HEAD_DIM = 64
PAIR = 2 * HEAD_DIM
EXTRA = 16
F32 = jnp.float32
BF16 = jnp.bfloat16
SCALE = HEAD_DIM ** (-0.5) * math.log2(math.e)


def dot(a, b):
    return jnp.dot(a, b, preferred_element_type=F32)


def kernel(
    n,
    lat_ref, cells_ref, wq_ref, wk_ref, wv_ref, wo_ref, wu_ref, wd_ref, out_ref,
    q, kz, vt, wus, wds,
    own, part, xin, zin, own_s, part_s, xin_s, zin_s,
    acc, att, att_in, upd, nrm, mown, mpart, mxin, mzin, macc,
    w_sem, q_zs, q_xs, q_r,
    p_zs, p_zr, p_xs, p_xr,
    ps_zs, ps_zr, ps_xs, ps_xr,
    a_sem, n_zs, n_xs, n_r, m_zs, m_zr, m_xs, m_xr,
):
    na = n // 2
    me = lax.axis_index("cell")
    head = lax.axis_index("head")
    a, b = me // 2, me % 2
    across = a * 2 + 1 - b
    heads = wq_ref.shape[1] // HEAD_DIM
    width = wq_ref.shape[1]
    half = out_ref.shape[0]
    count = cells_ref.shape[0]

    def peer(d):
        return (a + d) % na

    def send(src, dst, ss, rs, **where):
        return pltpu.make_async_remote_copy(
            src_ref=src, dst_ref=dst, send_sem=ss, recv_sem=rs,
            device_id=where, device_id_type=pl.DeviceIdType.MESH,
        )

    def each(low, high, f):
        def step(i, carry):
            f(i)
            return carry
        lax.fori_loop(low, high, step, 0)

    barrier = pltpu.get_barrier_semaphore()
    each(1, na, lambda d: pl.semaphore_signal(
        barrier, inc=1, device_id={"cell": peer(d) * 2 + b},
        device_id_type=pl.DeviceIdType.MESH))
    pl.semaphore_signal(barrier, inc=1, device_id={"cell": across},
                        device_id_type=pl.DeviceIdType.MESH)
    pl.semaphore_signal(barrier, inc=1, device_id={"head": 1 - head},
                        device_id_type=pl.DeviceIdType.MESH)
    q[me] = dot(lat_ref[...], wq_ref[...]).astype(BF16)
    pl.semaphore_wait(barrier, na + 1)

    def to_z(buf, zs, r, d):
        return send(buf.at[me], buf.at[me], zs.at[d], r.at[me], cell=peer(d) * 2 + b)

    def to_x(buf, xs, r, ap):
        slot = ap * 2 + b
        return send(buf.at[slot], buf.at[slot], xs.at[ap], r.at[slot], cell=across)

    def arrived(buf, xs, r, slot):
        send(buf.at[slot], buf.at[slot], xs.at[0], r.at[slot], cell=across).wait_recv()

    def gather_start(buf, zs, xs, r):
        to_x(buf, xs, r, a).start()
        each(1, na, lambda d: to_z(buf, zs, r, d).start())

    def forward(buf, xs, r, d):
        ap = peer(d)
        arrived(buf, xs, r, ap * 2 + b)
        to_x(buf, xs, r, ap).start()

    def gather_finish(buf, zs, xs, r):
        each(1, na, lambda d: to_z(buf, zs, r, d).wait_send())
        each(0, na, lambda ap: to_x(buf, xs, r, ap).wait_send())

    gather_start(q, q_zs, q_xs, q_r)
    up_copy = send(wu_ref, wus, w_sem.at[0], w_sem.at[1], head=1 - head)
    down_copy = send(wd_ref, wds, w_sem.at[2], w_sem.at[3], head=1 - head)
    up_copy.start()
    down_copy.start()

    tile = 256

    def project(t):
        rows = pl.ds(pl.multiple_of(t * tile, tile), tile)
        block = cells_ref[rows, :]
        k = dot(block, wk_ref[...]).astype(BF16)
        v = dot(block, wv_ref[...]).T.astype(BF16)
        lane = lax.broadcasted_iota(jnp.int32, (tile, PAIR), 1)
        for h in range(heads):
            pair = k[:, (h // 2) * PAIR:(h // 2 + 1) * PAIR]
            keep = (lane < HEAD_DIM) if h % 2 == 0 else (lane >= HEAD_DIM)
            kz[h, rows, :] = jnp.where(keep, pair, jnp.zeros_like(pair))
            vt[h, :HEAD_DIM, rows] = v[h * HEAD_DIM:(h + 1) * HEAD_DIM, :]
            vt[h, HEAD_DIM:, rows] = jnp.ones((EXTRA, tile), BF16)

    each(0, count // tile, project)

    def attend(slot, oref, sref, k):
        def pair_step(p):
            q2 = q[slot, :, pl.ds(pl.multiple_of(p * PAIR, PAIR), PAIR)]
            for e in range(2):
                h = 2 * p + e
                s = lax.dot_general(kz[h], q2, (((1,), (1,)), ((), ())),
                                    preferred_element_type=F32)
                m = jnp.max(s, axis=0, keepdims=True)
                w = jnp.exp2((s - m) * SCALE).astype(BF16)
                r = dot(vt[h], w)
                at = pl.ds(pl.multiple_of(h * HEAD_DIM, HEAD_DIM), HEAD_DIM)
                oref[k, at, :] = r[:HEAD_DIM].astype(BF16)
                sref[k, pl.ds(h, 1), :] = m * SCALE
                sref[k, pl.ds(heads + h, 1), :] = r[HEAD_DIM:HEAD_DIM + 1]
        each(0, heads // 2, pair_step)

    def part_to_x(ap):
        return (send(part.at[ap], xin.at[ap], p_xs.at[ap], p_xr.at[ap], cell=across),
                send(part_s.at[ap], xin_s.at[ap], ps_xs.at[ap], ps_xr.at[ap], cell=across))

    def own_to_z(ap, src):
        to = {"cell": ap * 2 + b}
        return (send(own.at[ap], zin.at[src], p_zs.at[ap], p_zr.at[src], **to),
                send(own_s.at[ap], zin_s.at[src], ps_zs.at[ap], ps_zr.at[src], **to))

    def weights_of(s1, s2):
        m1, l1, m2, l2 = s1[:heads], s1[heads:], s2[:heads], s2[heads:]
        m = jnp.maximum(m1, m2)
        e1, e2 = jnp.exp2(m1 - m), jnp.exp2(m2 - m)
        return e1, e2, jnp.concatenate([m, l1 * e1 + l2 * e2], axis=0)

    def spans():
        return [slice(h * HEAD_DIM, (h + 1) * HEAD_DIM) for h in range(heads)]

    def combine_and_send(d):
        ap = peer(d)
        for c in part_to_x(ap):
            c.wait_recv()
        e1, e2, stat = weights_of(own_s[ap], xin_s[ap])
        own_s[ap] = stat
        for h, at in enumerate(spans()):
            own[ap, at, :] = (own[ap, at, :].astype(F32) * e1[h:h + 1]
                              + xin[ap, at, :].astype(F32) * e2[h:h + 1]).astype(BF16)
        for c in own_to_z(ap, a):
            c.start()

    if na > 1:
        forward(q, q_xs, q_r, 1)
    attend(me, own, own_s, a)

    def step(d):
        ap = peer(d)
        arrived(q, q_xs, q_r, ap * 2 + 1 - b)
        attend(ap * 2 + 1 - b, part, part_s, ap)
        for c in part_to_x(ap):
            c.start()

        @pl.when(d + 1 < na)
        def _():
            forward(q, q_xs, q_r, d + 1)

        attend(ap * 2 + b, own, own_s, ap)

        @pl.when(d > 1)
        def _():
            combine_and_send(d - 1)

    each(1, na, step)
    arrived(q, q_xs, q_r, across)
    if na > 1:
        combine_and_send(na - 1)
    attend(across, part, part_s, a)
    for c in part_to_x(a):
        c.start()

    for at in spans():
        acc[at, :] = own[a, at, :].astype(F32)

    def merge(o_ref, s_ref, k):
        e1, e2, stat = weights_of(own_s[a], s_ref[k])
        own_s[a] = stat
        for h, at in enumerate(spans()):
            acc[at, :] = acc[at, :] * e1[h:h + 1] + o_ref[k, at, :].astype(F32) * e2[h:h + 1]

    def from_z(d):
        ap = peer(na - d)
        for c in own_to_z(ap, ap):
            c.wait_recv()
        merge(zin, zin_s, ap)

    each(1, na, from_z)
    for c in part_to_x(a):
        c.wait_recv()
    merge(xin, xin_s, a)
    totals = own_s[a, heads:, :]
    for h, at in enumerate(spans()):
        acc[at, :] = acc[at, :] / totals[h:h + 1]
    att[...] = acc[...].T.astype(BF16).reshape(2, half, width)

    swap = send(att.at[1 - head], att_in, a_sem.at[0], a_sem.at[1], head=1 - head)
    swap.start()
    own_rows = pl.ds(pl.multiple_of(head * half, half), half)
    first = pl.ds(pl.multiple_of(head * width, width), width)
    second = pl.ds(pl.multiple_of((1 - head) * width, width), width)
    projected = dot(att[head], wo_ref[first, :])
    swap.wait_recv()
    projected = projected + dot(att_in[...], wo_ref[second, :])
    updated = (lat_ref[own_rows, :].astype(F32) + projected).astype(BF16).astype(F32)
    upd[...] = updated
    nrm[me] = (updated * lax.rsqrt(jnp.mean(updated * updated, axis=1, keepdims=True) + 1e-5)
               ).astype(BF16)

    gather_start(nrm, n_zs, n_xs, n_r)
    up_copy.wait_recv()
    down_copy.wait_recv()

    def mlp(slot):
        x = nrm[slot]
        h1 = jax.nn.gelu(dot(x, wu_ref[...]), approximate=True).astype(BF16)
        h2 = jax.nn.gelu(dot(x, wus[...]), approximate=True).astype(BF16)
        return dot(h1, wd_ref[...]) + dot(h2, wds[...])

    def mlp_to_x(ap):
        return send(mpart.at[ap], mxin.at[ap], m_xs.at[ap], m_xr.at[ap], cell=across)

    def mlp_to_z(ap, src):
        return send(mown.at[ap], mzin.at[src], m_zs.at[ap], m_zr.at[src], cell=ap * 2 + b)

    def mlp_combine(d):
        ap = peer(d)
        mlp_to_x(ap).wait_recv()
        mown[ap] = (mown[ap].astype(F32) + mxin[ap].astype(F32)).astype(BF16)
        mlp_to_z(ap, a).start()

    macc[...] = upd[...] + mlp(me)

    def mlp_step(d):
        ap = peer(d)
        forward(nrm, n_xs, n_r, d)
        mown[ap] = mlp(ap * 2 + b).astype(BF16)
        arrived(nrm, n_xs, n_r, ap * 2 + 1 - b)
        mpart[ap] = mlp(ap * 2 + 1 - b).astype(BF16)
        mlp_to_x(ap).start()

        @pl.when(d > 1)
        def _():
            mlp_combine(d - 1)

    each(1, na, mlp_step)
    arrived(nrm, n_xs, n_r, across)
    mpart[a] = mlp(across).astype(BF16)
    mlp_to_x(a).start()
    if na > 1:
        mlp_combine(na - 1)
    mlp_to_x(a).wait_recv()
    macc[...] += mxin[a].astype(F32)

    def mlp_from_z(d):
        ap = peer(na - d)
        mlp_to_z(ap, ap).wait_recv()
        macc[...] += mzin[ap].astype(F32)

    each(1, na, mlp_from_z)
    out_ref[...] = macc[...].astype(BF16)

    gather_finish(q, q_zs, q_xs, q_r)
    gather_finish(nrm, n_zs, n_xs, n_r)
    up_copy.wait_send()
    down_copy.wait_send()
    swap.wait_send()

    def drain_x(ap):
        for c in part_to_x(ap):
            c.wait_send()
        mlp_to_x(ap).wait_send()

    def drain_z(d):
        for c in own_to_z(peer(d), a):
            c.wait_send()
        mlp_to_z(peer(d), a).wait_send()

    each(0, na, drain_x)
    each(1, na, drain_z)


def body(latents, cells, w_query, w_key, w_value, w_out, w_up, w_down):
    n = lax.axis_size("cell")
    na = n // 2
    rows, dim = latents.shape
    half = rows // lax.axis_size("head")
    width = w_query.shape[1]
    heads = width // HEAD_DIM
    count = cells.shape[0]
    vmem = pl.BlockSpec(memory_space=pltpu.VMEM)
    dma = pltpu.SemaphoreType.DMA
    partial = pltpu.VMEM((na, width, rows), BF16)
    stats = pltpu.VMEM((na, 2 * heads, rows), F32)
    mlp_part = pltpu.VMEM((na, half, dim), BF16)
    return pl.pallas_call(
        functools.partial(kernel, n),
        out_shape=jax.ShapeDtypeStruct((half, dim), BF16),
        in_specs=[vmem] * 8,
        out_specs=vmem,
        scratch_shapes=[
            pltpu.VMEM((n, rows, width), BF16),
            pltpu.VMEM((heads, count, PAIR), BF16),
            pltpu.VMEM((heads, HEAD_DIM + EXTRA, count), BF16),
            pltpu.VMEM(w_up.shape, BF16),
            pltpu.VMEM(w_down.shape, BF16),
            partial, partial, partial, partial,
            stats, stats, stats, stats,
            pltpu.VMEM((width, rows), F32),
            pltpu.VMEM((2, half, width), BF16),
            pltpu.VMEM((half, width), BF16),
            pltpu.VMEM((half, dim), F32),
            pltpu.VMEM((n, half, dim), BF16),
            mlp_part, mlp_part, mlp_part, mlp_part,
            pltpu.VMEM((half, dim), F32),
            dma((4,)), dma((na,)), dma((na,)), dma((n,)),
            dma((na,)), dma((na,)), dma((na,)), dma((na,)),
            dma((na,)), dma((na,)), dma((na,)), dma((na,)),
            dma((2,)), dma((na,)), dma((na,)), dma((n,)),
            dma((na,)), dma((na,)), dma((na,)), dma((na,)),
        ],
        compiler_params=pltpu.CompilerParams(
            collective_id=0, has_side_effects=True, vmem_limit_bytes=58 * 1024 * 1024
        ),
        cost_estimate=pl.CostEstimate(
            flops=12_000_000_000, bytes_accessed=9_000_000, transcendentals=17_000_000
        ),
    )(latents, cells, w_query, w_key, w_value, w_out, w_up, w_down)


def solution(mesh):
    return jax.shard_map(
        body,
        mesh=mesh,
        in_specs=(
            P(("group", "cell"), None),
            P(("group", "cell"), None),
            P(None, "head"),
            P(None, "head"),
            P(None, "head"),
            P(),
            P(None, ("cell", "head")),
            P(("cell", "head"), None),
        ),
        out_specs=P(("group", "cell", "head"), None),
        check_vma=False,
    )
```

time: 474 us -> 174 us (0.37)
  waiting for transfers between devices: 272 us -> 0 us
  Pallas kernels: 0 us -> 172 us
  matrix products: 81.5 us -> 0 us
  other arithmetic: 39.7 us -> 0 us
  blocking collectives: 38.7 us -> 0 us
  local copies, waits for them, and re-layouts: 22.8 us -> 1.67 us
  between operations: 14.9 us -> 0.01 us
    psum x1 -> x0, waiting for transfers between devices: 221 us -> none  [body(): summed_out, summed_tot = lax.psum((scaled_out, scaled_tot), 'cell')]
    pallas_call x0 -> x1, Pallas kernels: none -> 172 us  [body(): pl.pallas_call(functools.partial(kernel, n), out_shape=jax.ShapeDtypeStru...]
    dot_general x13 -> x0, matrix products: 81.5 us -> none  [the longest x4 32.5 us: pair_partial(): jnp.einsum('lhd,chd->hlc', query_pair, key_pair, preferred_element_type=j...]
    all_gather x3 -> x0, waiting for transfers between devices: 50.2 us -> none  [the longest x1 46.4 us: body(): queries = lax.all_gather(local_queries, 'cell', axis=0, tiled=True)]
    pmax x1 -> x0, blocking collectives: 34.7 us -> none  [body(): lax.pmax(block_max.astype(jnp.bfloat16), 'cell').astype(block_max.dtype)]
    reduce_sum x4 -> x0, other arithmetic: 34 us -> none  [pair_partial(): totals = jnp.sum(weights, axis=2)]
    dynamic_slice x29 -> x0, local copies, waits for them, and re-layouts: 17.5 us -> none  [the longest x24 14.1 us: pair_slice(): lax.dynamic_slice_in_dim(matrix, pair_index * pair_width, pair_width, 1)]
    mul x2 -> x0, other arithmetic: 5.55 us -> none  [the longest x1 4.85 us: body(): partial_out.reshape(pair_count, latent_count, 2, HEAD_DIM)]
  transfers between devices with their start and end apart: 4 -> 0, of which waited for: 3 -> 0; matrix products, arithmetic and copies ran while one was open for 2% -> 0% of each run, Pallas kernels for 0% -> 0%
where the time goes in v1:
time: 174 us
  Pallas kernels  172 us (99%)
    pallas_call x1, Pallas kernels, body(): pl.pallas_call(functools.partial(kernel, n), out_shape=jax.ShapeDtypeStru...  172 us

profile of v1, /device:TPU:0, one launch (start us, length us, event | category | flops | bytes accessed | tf_op | source)
XLA Modules:
  0.0 173.9 jit_solution(11793824897126195262)
XLA Ops:
  0.0 172.2 %shard_map.82 = bf16[128,1024]{1,0:T(8,128)(2,1)} custom-call(bf16[256,1024]{1,0:T(8,128)(2,1)} %lat_ref.1, bf16[1024,1024]{1,0:T(8,128)(2,1)} %cells_ref.1, bf16[1024,512]{1,0:T(8,128)(2,1)} %wq_ref.1, bf16[1024,512]{1,0:T(8,128)(2,1)} %wk_ref.1, bf16[1024,512]{1,0:T(8,128)(2,1)} %wv_ref.1, bf16[1024,1024]{1,0:T(8,128)(2,1)} %wo_ref.1, ...), custom_call_target="tpu_custom_call" | custom-call | flops 12000000000 | bytes 9000000 | tf_op jit(solution)/shard_map/pallas_call | solution.py:314
  172.2 1.7 copy.10

commit v2 on v1

v2 whole, which is shorter than its diff:
```python
import functools
import math

import jax
import jax.numpy as jnp
from jax import lax
from jax.experimental import pallas as pl
from jax.experimental.pallas import tpu as pltpu
from jax.sharding import PartitionSpec as P

HEAD_DIM = 64
PAIR = 2 * HEAD_DIM
EXTRA = 16
F32 = jnp.float32
BF16 = jnp.bfloat16
SCALE = HEAD_DIM ** (-0.5) * math.log2(math.e)


def dot(a, b):
    return jnp.dot(a, b, preferred_element_type=F32)


def kernel(
    n,
    lat_ref, cells_ref, wq_ref, wk_ref, wv_ref, wo_ref, wu_ref, wd_ref, out_ref,
    q, cin, kz, vt, wus, wds,
    own, part, zin, own_s, part_s, zin_s,
    acc, att, att_in, nrm, mown, mzin, macc,
    c_sem, w_sem, q_s, q_r, p_s, p_r, ps_s, ps_r, a_sem, n_s, n_r, m_s, m_r,
):
    na = n // 2
    me = lax.axis_index("cell")
    head = lax.axis_index("head")
    a, b = me // 2, me % 2
    across = a * 2 + 1 - b
    heads = wq_ref.shape[1] // HEAD_DIM
    width = wq_ref.shape[1]
    half = out_ref.shape[0]
    count = cells_ref.shape[0]

    def peer(d):
        return (a + d) % na

    def send(src, dst, ss, rs, **where):
        return pltpu.make_async_remote_copy(
            src_ref=src, dst_ref=dst, send_sem=ss, recv_sem=rs,
            device_id=where, device_id_type=pl.DeviceIdType.MESH,
        )

    def each(low, high, f):
        def step(i, carry):
            f(i)
            return carry
        lax.fori_loop(low, high, step, 0)

    barrier = pltpu.get_barrier_semaphore()
    each(1, na, lambda d: pl.semaphore_signal(
        barrier, inc=1, device_id={"cell": peer(d) * 2 + b},
        device_id_type=pl.DeviceIdType.MESH))
    pl.semaphore_signal(barrier, inc=1, device_id={"cell": across},
                        device_id_type=pl.DeviceIdType.MESH)
    pl.semaphore_signal(barrier, inc=1, device_id={"head": 1 - head},
                        device_id_type=pl.DeviceIdType.MESH)
    q[a] = dot(lat_ref[...], wq_ref[...]).astype(BF16)
    pl.semaphore_wait(barrier, na + 1)

    def across_x(src, dst, ss, rs):
        return send(src, dst, ss, rs, cell=across)

    def to_sibling(src, dst, ss, rs):
        return send(src, dst, ss, rs, head=1 - head)

    cell_half = count // 2
    cell_rows = pl.ds(pl.multiple_of(head * cell_half, cell_half), cell_half)
    cells_x = across_x(cells_ref.at[cell_rows], cin.at[head], c_sem.at[0], c_sem.at[1])
    cells_fwd = to_sibling(cin.at[head], cin.at[head], c_sem.at[2], c_sem.at[3])
    cells_from = to_sibling(cin.at[1 - head], cin.at[1 - head], c_sem.at[2], c_sem.at[3])
    up_s = to_sibling(wu_ref, wus.at[0], w_sem.at[0], w_sem.at[1])
    down_s = to_sibling(wd_ref, wds.at[0], w_sem.at[2], w_sem.at[3])
    up_x = across_x(wu_ref, wus.at[1], w_sem.at[4], w_sem.at[5])
    down_x = across_x(wd_ref, wds.at[1], w_sem.at[6], w_sem.at[7])
    up_f = to_sibling(wus.at[1], wus.at[2], w_sem.at[8], w_sem.at[9])
    down_f = to_sibling(wds.at[1], wds.at[2], w_sem.at[10], w_sem.at[11])

    def to_z(buf, ss, r, d):
        return send(buf.at[a], buf.at[a], ss.at[d], r.at[a], cell=peer(d) * 2 + b)

    def arrived(buf, r, ap):
        send(buf.at[ap], buf.at[ap], r.at[ap], r.at[ap], cell=across).wait_recv()

    cells_x.start()
    each(1, na, lambda d: to_z(q, q_s, q_r, d).start())
    up_s.start()
    down_s.start()

    tile = 256

    def project(block, t, side):
        rows = pl.ds(pl.multiple_of(t * tile, tile), tile)
        k = dot(block, wk_ref[...]).astype(BF16)
        v = dot(block, wv_ref[...]).T.astype(BF16)
        lane = lax.broadcasted_iota(jnp.int32, (tile, PAIR), 1)
        for h in range(heads):
            pair = k[:, (h // 2) * PAIR:(h // 2 + 1) * PAIR]
            keep = (lane < HEAD_DIM) if h % 2 == 0 else (lane >= HEAD_DIM)
            kz[side * heads + h, rows, :] = jnp.where(keep, pair, jnp.zeros_like(pair))
            vt[side * heads + h, :HEAD_DIM, rows] = v[h * HEAD_DIM:(h + 1) * HEAD_DIM, :]
            vt[side * heads + h, HEAD_DIM:, rows] = jnp.ones((EXTRA, tile), BF16)

    def rows_at(t):
        return pl.ds(pl.multiple_of(t * tile, tile), tile)

    each(0, count // tile, lambda t: project(cells_ref[rows_at(t), :], t, 0))

    def attend(side, oref, sref, k):
        def pair_step(p):
            q2 = q[k, :, pl.ds(pl.multiple_of(p * PAIR, PAIR), PAIR)]
            for e in range(2):
                h = 2 * p + e
                s = lax.dot_general(kz[side * heads + h], q2, (((1,), (1,)), ((), ())),
                                    preferred_element_type=F32)
                m = jnp.max(s, axis=0, keepdims=True)
                w = jnp.exp2((s - m) * SCALE).astype(BF16)
                r = dot(vt[side * heads + h], w)
                at = pl.ds(pl.multiple_of(h * HEAD_DIM, HEAD_DIM), HEAD_DIM)
                oref[k, at, :] = r[:HEAD_DIM].astype(BF16)
                sref[k, pl.ds(h, 1), :] = m * SCALE
                sref[k, pl.ds(heads + h, 1), :] = r[HEAD_DIM:HEAD_DIM + 1]
        each(0, heads // 2, pair_step)

    def own_to_z(ap, src):
        to = {"cell": ap * 2 + b}
        return (send(own.at[ap], zin.at[src], p_s.at[ap], p_r.at[src], **to),
                send(own_s.at[ap], zin_s.at[src], ps_s.at[ap], ps_r.at[src], **to))

    def weights_of(s1, s2):
        m1, l1, m2, l2 = s1[:heads], s1[heads:], s2[:heads], s2[heads:]
        m = jnp.maximum(m1, m2)
        e1, e2 = jnp.exp2(m1 - m), jnp.exp2(m2 - m)
        return e1, e2, jnp.concatenate([m, l1 * e1 + l2 * e2], axis=0)

    def spans():
        return [slice(h * HEAD_DIM, (h + 1) * HEAD_DIM) for h in range(heads)]

    attend(0, own, own_s, a)

    def first_side(d):
        ap = peer(d)
        arrived(q, q_r, ap)
        attend(0, own, own_s, ap)

        @pl.when(d == 1)
        def _():
            cells_x.wait_recv()
            cells_fwd.start()
            up_x.start()
            down_x.start()

    each(1, na, first_side)

    def project_in(i):
        side = i // (cell_half // tile)
        at = i % (cell_half // tile)
        project(cin[side, rows_at(at), :], i, 1)

    cells_from.wait_recv()
    each(0, count // tile, project_in)

    def second_side(d):
        ap = peer(d)
        attend(1, part, part_s, ap)
        e1, e2, stat = weights_of(own_s[ap], part_s[ap])
        own_s[ap] = stat
        for h, at in enumerate(spans()):
            own[ap, at, :] = (own[ap, at, :].astype(F32) * e1[h:h + 1]
                              + part[ap, at, :].astype(F32) * e2[h:h + 1]).astype(BF16)
        for c in own_to_z(ap, a):
            c.start()

    each(1, na, second_side)
    up_x.wait_recv()
    down_x.wait_recv()
    up_f.start()
    down_f.start()
    attend(1, part, part_s, a)

    for at in spans():
        acc[at, :] = own[a, at, :].astype(F32)

    def merge(o_ref, s_ref, k):
        e1, e2, stat = weights_of(own_s[a], s_ref[k])
        own_s[a] = stat
        for h, at in enumerate(spans()):
            acc[at, :] = acc[at, :] * e1[h:h + 1] + o_ref[k, at, :].astype(F32) * e2[h:h + 1]

    merge(part, part_s, a)

    def from_z(d):
        ap = peer(na - d)
        for c in own_to_z(ap, ap):
            c.wait_recv()
        merge(zin, zin_s, ap)

    each(1, na, from_z)
    totals = own_s[a, heads:, :]
    for h, at in enumerate(spans()):
        acc[at, :] = acc[at, :] / totals[h:h + 1]
    att[...] = acc[...].T.astype(BF16).reshape(2, half, width)

    swap = to_sibling(att.at[1 - head], att_in, a_sem.at[0], a_sem.at[1])
    swap.start()
    own_rows = pl.ds(pl.multiple_of(head * half, half), half)
    first = pl.ds(pl.multiple_of(head * width, width), width)
    second = pl.ds(pl.multiple_of((1 - head) * width, width), width)
    projected = dot(att[head], wo_ref[first, :])
    swap.wait_recv()
    projected = projected + dot(att_in[...], wo_ref[second, :])
    updated = (lat_ref[own_rows, :].astype(F32) + projected).astype(BF16).astype(F32)
    macc[...] = updated
    nrm[a] = (updated * lax.rsqrt(jnp.mean(updated * updated, axis=1, keepdims=True) + 1e-5)
              ).astype(BF16)
    each(1, na, lambda d: to_z(nrm, n_s, n_r, d).start())
    for c in (up_s, down_s, up_f, down_f):
        c.wait_recv()

    def mlp(slot):
        x = nrm[slot]
        hid = jax.nn.gelu(dot(x, wu_ref[...]), approximate=True).astype(BF16)
        total = dot(hid, wd_ref[...])
        for i in range(3):
            hid = jax.nn.gelu(dot(x, wus[i]), approximate=True).astype(BF16)
            total = total + dot(hid, wds[i])
        return total

    def mlp_to_z(ap, src):
        return send(mown.at[ap], mzin.at[src], m_s.at[ap], m_r.at[src], cell=ap * 2 + b)

    def mlp_step(d):
        ap = peer(d)
        arrived(nrm, n_r, ap)
        mown[ap] = mlp(ap).astype(BF16)
        mlp_to_z(ap, a).start()

    macc[...] += mlp(a)
    each(1, na, mlp_step)

    def mlp_from_z(d):
        ap = peer(na - d)
        mlp_to_z(ap, ap).wait_recv()
        macc[...] += mzin[ap].astype(F32)

    each(1, na, mlp_from_z)
    out_ref[...] = macc[...].astype(BF16)

    for c in (cells_x, cells_fwd, up_s, down_s, up_x, down_x, up_f, down_f, swap):
        c.wait_send()

    def drain(d):
        to_z(q, q_s, q_r, d).wait_send()
        to_z(nrm, n_s, n_r, d).wait_send()
        for c in own_to_z(peer(d), a):
            c.wait_send()
        mlp_to_z(peer(d), a).wait_send()

    each(1, na, drain)


def body(latents, cells, w_query, w_key, w_value, w_out, w_up, w_down):
    n = lax.axis_size("cell")
    na = n // 2
    rows, dim = latents.shape
    half = rows // lax.axis_size("head")
    width = w_query.shape[1]
    heads = width // HEAD_DIM
    count = cells.shape[0]
    vmem = pl.BlockSpec(memory_space=pltpu.VMEM)
    dma = pltpu.SemaphoreType.DMA
    partial = pltpu.VMEM((na, width, rows), BF16)
    stats = pltpu.VMEM((na, 2 * heads, rows), F32)
    mlp_part = pltpu.VMEM((na, half, dim), BF16)
    return pl.pallas_call(
        functools.partial(kernel, n),
        out_shape=jax.ShapeDtypeStruct((half, dim), BF16),
        in_specs=[vmem] * 8,
        out_specs=vmem,
        scratch_shapes=[
            pltpu.VMEM((na, rows, width), BF16),
            pltpu.VMEM((2, count // 2, dim), BF16),
            pltpu.VMEM((2 * heads, count, PAIR), BF16),
            pltpu.VMEM((2 * heads, HEAD_DIM + EXTRA, count), BF16),
            pltpu.VMEM((3,) + w_up.shape, BF16),
            pltpu.VMEM((3,) + w_down.shape, BF16),
            partial, partial, partial,
            stats, stats, stats,
            pltpu.VMEM((width, rows), F32),
            pltpu.VMEM((2, half, width), BF16),
            pltpu.VMEM((half, width), BF16),
            pltpu.VMEM((na, half, dim), BF16),
            mlp_part, mlp_part,
            pltpu.VMEM((half, dim), F32),
            dma((4,)), dma((12,)), dma((na,)), dma((na,)),
            dma((na,)), dma((na,)), dma((na,)), dma((na,)), dma((2,)),
            dma((na,)), dma((na,)), dma((na,)), dma((na,)),
        ],
        compiler_params=pltpu.CompilerParams(
            collective_id=0, has_side_effects=True, vmem_limit_bytes=58 * 1024 * 1024
        ),
        cost_estimate=pl.CostEstimate(
            flops=12_000_000_000, bytes_accessed=9_000_000, transcendentals=17_000_000
        ),
    )(latents, cells, w_query, w_key, w_value, w_out, w_up, w_down)


def solution(mesh):
    return jax.shard_map(
        body,
        mesh=mesh,
        in_specs=(
            P(("group", "cell"), None),
            P(("group", "cell"), None),
            P(None, "head"),
            P(None, "head"),
            P(None, "head"),
            P(),
            P(None, ("cell", "head")),
            P(("cell", "head"), None),
        ),
        out_specs=P(("group", "cell", "head"), None),
        check_vma=False,
    )
```

time: 174 us -> 132 us (0.76)
  the two profiles are of different devices: /device:TPU:0 before, /device:TPU:25 now
where the time goes in v2:
time: 132 us
  Pallas kernels  130 us (98%)
  local copies, waits for them, and re-layouts  1.67 us (1%)
    pallas_call x1, Pallas kernels, body(): pl.pallas_call(functools.partial(kernel, n), out_shape=jax.ShapeDtypeStru...  130 us

profile of v2, /device:TPU:25, one launch (start us, length us, event | category | flops | bytes accessed | tf_op | source)
XLA Modules:
  0.0 132.0 jit_solution(10579588518594767482)
XLA Ops:
  0.0 130.3 %shard_map.82 = bf16[128,1024]{1,0:T(8,128)(2,1)} custom-call(bf16[256,1024]{1,0:T(8,128)(2,1)} %lat_ref.1, bf16[1024,1024]{1,0:T(8,128)(2,1)} %cells_ref.1, bf16[1024,512]{1,0:T(8,128)(2,1)} %wq_ref.1, bf16[1024,512]{1,0:T(8,128)(2,1)} %wk_ref.1, bf16[1024,512]{1,0:T(8,128)(2,1)} %wv_ref.1, bf16[1024,1024]{1,0:T(8,128)(2,1)} %wo_ref.1, ...), custom_call_target="tpu_custom_call" | custom-call | flops 12000000000 | bytes 9000000 | tf_op jit(solution)/shard_map/pallas_call | solution.py:281
  130.3 1.7 %copy.10 = bf16[128,1024]{1,0:T(8,128)(2,1)} copy(bf16[128,1024]{1,0:T(8,128)(2,1)} %shard_map.82) | data formatting | bytes 524288

commit v3 on v2

--- a/solution.py
+++ b/solution.py
@@ -82,14 +82,50 @@
     up_f = to_sibling(wus.at[1], wus.at[2], w_sem.at[8], w_sem.at[9])
     down_f = to_sibling(wds.at[1], wds.at[2], w_sem.at[10], w_sem.at[11])
 
-    def to_z(buf, ss, r, d):
-        return send(buf.at[a], buf.at[a], ss.at[d], r.at[a], cell=peer(d) * 2 + b)
+    def up_z(buf, ss, r, j):
+        return send(buf.at[j], buf.at[j], ss.at[j], r.at[j], cell=me + 2)
+
+    def down_z(buf, ss, r, j):
+        return send(buf.at[j], buf.at[j], ss.at[na + j], r.at[j], cell=me - 2)
+
+    def pass_on(buf, ss, r, j, rising, falling):
+        if rising:
+            @pl.when(a + 1 < na)
+            def _():
+                up_z(buf, ss, r, j).start()
+        if falling:
+            @pl.when(a > 0)
+            def _():
+                down_z(buf, ss, r, j).start()
+
+    def line_step(buf, ss, r, k, work):
+        @pl.when(a >= k)
+        def _():
+            arrived(buf, r, a - k)
+            pass_on(buf, ss, r, a - k, True, False)
+
+        @pl.when(a + k < na)
+        def _():
+            arrived(buf, r, a + k)
+            pass_on(buf, ss, r, a + k, False, True)
+
+        pl.when(a >= k)(lambda: work(a - k))
+        pl.when(a + k < na)(lambda: work(a + k))
+
+    def line_finish(buf, ss, r):
+        @pl.when(a + 1 < na)
+        def _():
+            each(0, a + 1, lambda j: up_z(buf, ss, r, j).wait_send())
+
+        @pl.when(a > 0)
+        def _():
+            each(a, na, lambda j: down_z(buf, ss, r, j).wait_send())
 
     def arrived(buf, r, ap):
         send(buf.at[ap], buf.at[ap], r.at[ap], r.at[ap], cell=across).wait_recv()
 
     cells_x.start()
-    each(1, na, lambda d: to_z(q, q_s, q_r, d).start())
+    pass_on(q, q_s, q_r, a, True, True)
     up_s.start()
     down_s.start()
 
@@ -144,19 +180,11 @@
 
     attend(0, own, own_s, a)
 
-    def first_side(d):
-        ap = peer(d)
-        arrived(q, q_r, ap)
-        attend(0, own, own_s, ap)
-
-        @pl.when(d == 1)
-        def _():
-            cells_x.wait_recv()
-            cells_fwd.start()
-            up_x.start()
-            down_x.start()
-
-    each(1, na, first_side)
+    each(1, na, lambda k: line_step(q, q_s, q_r, k, lambda j: attend(0, own, own_s, j)))
+    cells_x.wait_recv()
+    cells_fwd.start()
+    up_x.start()
+    down_x.start()
 
     def project_in(i):
         side = i // (cell_half // tile)
@@ -219,7 +247,7 @@
     macc[...] = updated
     nrm[a] = (updated * lax.rsqrt(jnp.mean(updated * updated, axis=1, keepdims=True) + 1e-5)
               ).astype(BF16)
-    each(1, na, lambda d: to_z(nrm, n_s, n_r, d).start())
+    pass_on(nrm, n_s, n_r, a, True, True)
     for c in (up_s, down_s, up_f, down_f):
         c.wait_recv()
 
@@ -235,14 +263,12 @@
     def mlp_to_z(ap, src):
         return send(mown.at[ap], mzin.at[src], m_s.at[ap], m_r.at[src], cell=ap * 2 + b)
 
-    def mlp_step(d):
-        ap = peer(d)
-        arrived(nrm, n_r, ap)
+    def mlp_step(ap):
         mown[ap] = mlp(ap).astype(BF16)
         mlp_to_z(ap, a).start()
 
     macc[...] += mlp(a)
-    each(1, na, mlp_step)
+    each(1, na, lambda k: line_step(nrm, n_s, n_r, k, mlp_step))
 
     def mlp_from_z(d):
         ap = peer(na - d)
@@ -256,13 +282,13 @@
         c.wait_send()
 
     def drain(d):
-        to_z(q, q_s, q_r, d).wait_send()
-        to_z(nrm, n_s, n_r, d).wait_send()
         for c in own_to_z(peer(d), a):
             c.wait_send()
         mlp_to_z(peer(d), a).wait_send()
 
     each(1, na, drain)
+    line_finish(q, q_s, q_r)
+    line_finish(nrm, n_s, n_r)
 
 
 def body(latents, cells, w_query, w_key, w_value, w_out, w_up, w_down):
@@ -298,9 +324,9 @@
             pltpu.VMEM((na, half, dim), BF16),
             mlp_part, mlp_part,
             pltpu.VMEM((half, dim), F32),
-            dma((4,)), dma((12,)), dma((na,)), dma((na,)),
+            dma((4,)), dma((12,)), dma((2 * na,)), dma((na,)),
             dma((na,)), dma((na,)), dma((na,)), dma((na,)), dma((2,)),
-            dma((na,)), dma((na,)), dma((na,)), dma((na,)),
+            dma((2 * na,)), dma((na,)), dma((na,)), dma((na,)),
         ],
         compiler_params=pltpu.CompilerParams(
             collective_id=0, has_side_effects=True, vmem_limit_bytes=58 * 1024 * 1024

time: 132 us -> 128 us (0.970)
  the two profiles are of different devices: /device:TPU:25 before, /device:TPU:0 now
where the time goes in v3:
time: 128 us
  Pallas kernels  126 us (98%)
  local copies, waits for them, and re-layouts  1.67 us (1%)
    pallas_call x1, Pallas kernels, body(): pl.pallas_call(functools.partial(kernel, n), out_shape=jax.ShapeDtypeStru...  126 us

profile of v3, /device:TPU:0, one launch (start us, length us, event | category | flops | bytes accessed | tf_op | source)
XLA Modules:
  0.0 127.8 jit_solution(8245729725016792110)
XLA Ops:
  0.0 126.1 %shard_map.82 = bf16[128,1024]{1,0:T(8,128)(2,1)} custom-call(bf16[256,1024]{1,0:T(8,128)(2,1)} %lat_ref.1, bf16[1024,1024]{1,0:T(8,128)(2,1)} %cells_ref.1, bf16[1024,512]{1,0:T(8,128)(2,1)} %wq_ref.1, bf16[1024,512]{1,0:T(8,128)(2,1)} %wk_ref.1, bf16[1024,512]{1,0:T(8,128)(2,1)} %wv_ref.1, bf16[1024,1024]{1,0:T(8,128)(2,1)} %wo_ref.1, ...), custom_call_target="tpu_custom_call" | custom-call | flops 12000000000 | bytes 9000000 | tf_op jit(solution)/shard_map/pallas_call | solution.py:307
  126.1 1.7 %copy.10 = bf16[128,1024]{1,0:T(8,128)(2,1)} copy(bf16[128,1024]{1,0:T(8,128)(2,1)} %shard_map.82) | data formatting | bytes 524288

commit v4 on v3

--- a/solution.py
+++ b/solution.py
@@ -195,7 +195,7 @@
     each(0, count // tile, project_in)
 
     def second_side(d):
-        ap = peer(d)
+        ap = (a + jnp.where(a < na // 2, na - d, d)) % na
         attend(1, part, part_s, ap)
         e1, e2, stat = weights_of(own_s[ap], part_s[ap])
         own_s[ap] = stat

time: 128 us -> 125 us (0.977)
  Pallas kernels: 126 us -> 124 us
    pallas_call x1, Pallas kernels: 126 us -> 124 us  [body(): pl.pallas_call(functools.partial(kernel, n), out_shape=jax.ShapeDtypeStru...]
where the time goes in v4:
time: 125 us
  Pallas kernels  124 us (99%)
  local copies, waits for them, and re-layouts  1.67 us (1%)
    pallas_call x1, Pallas kernels, body(): pl.pallas_call(functools.partial(kernel, n), out_shape=jax.ShapeDtypeStru...  124 us

profile of v4, /device:TPU:0, one launch (start us, length us, event | category | flops | bytes accessed | tf_op | source)
XLA Modules:
  0.0 125.3 jit_solution(10390092478081314450)
XLA Ops:
  0.0 123.6 %shard_map.82 = bf16[128,1024]{1,0:T(8,128)(2,1)} custom-call(bf16[256,1024]{1,0:T(8,128)(2,1)} %lat_ref.1, bf16[1024,1024]{1,0:T(8,128)(2,1)} %cells_ref.1, bf16[1024,512]{1,0:T(8,128)(2,1)} %wq_ref.1, bf16[1024,512]{1,0:T(8,128)(2,1)} %wk_ref.1, bf16[1024,512]{1,0:T(8,128)(2,1)} %wv_ref.1, bf16[1024,1024]{1,0:T(8,128)(2,1)} %wo_ref.1, ...), custom_call_target="tpu_custom_call" | custom-call | flops 12000000000 | bytes 9000000 | tf_op jit(solution)/shard_map/pallas_call | solution.py:307
  123.6 1.7 %copy.10 = bf16[128,1024]{1,0:T(8,128)(2,1)} copy(bf16[128,1024]{1,0:T(8,128)(2,1)} %shard_map.82) | data formatting | bytes 524288
